TPU v7x, 32 devices: a whole 2x2x4 slice. The times are simulated.
32 devices in a mesh: group: 2 (over y), view: 4 (over z), tok: 4 (over x, core).
Axes of the slice: x: 2, y: 2, z: 4, core: 2. Of those that a mesh axis runs over, the one named last changes fastest.
Arguments:
- query_rows: bfloat16 [8192, 384], P(('group', 'view', 'tok')), parts along dimension 0, may hold values from -6 to 6
- key_rows: bfloat16 [8192, 384], P(('group', 'view', 'tok')), parts along dimension 0, may hold values from -6 to 6
- value_rows: bfloat16 [8192, 384], P(('group', 'view', 'tok')), parts along dimension 0, may hold values from -6 to 6
- token_rates: float32 [8192], P(('group', 'view', 'tok')), parts along dimension 0, may hold values from 0.25 to 4
- output_cot: bfloat16 [8192, 384], P(('group', 'view', 'tok')), parts along dimension 0, may hold values from -6 to 6
- w_gate: float32 [768, 384], replicated, may hold values from -0.3125 to 0.3125
- w_up: float32 [768, 384], replicated, may hold values from -0.3125 to 0.3125
- w_down: float32 [768, 384], replicated, may hold values from -0.21875 to 0.21875
Outputs:
- queries_grad: bfloat16 [8192, 384], P(('group', 'view', 'tok')), parts along dimension 0
- keys_grad: bfloat16 [8192, 384], P(('group', 'view', 'tok')), parts along dimension 0
- values_grad: bfloat16 [8192, 384], P(('group', 'view', 'tok')), parts along dimension 0
- rates_grad: float32 [8192], P(('group', 'view', 'tok')), parts along dimension 0
There are 2 independent parts, one for each index of `group`. A program takes and returns all parts, laid end to end along the dimension named above; an argument that names none is the same for every part. Nothing has to cross between parts.
All inputs are finite; a program needn't handle non-finite values.
Results may differ from a plain program's by a relative error of at most 0.015.
Values may be sent and summed in bfloat16 or wider, within the bound.
A program may use at most 128 MiB of HBM per device.

v0:
```python
import jax
import jax.numpy as jnp
from jax import lax
from jax.sharding import PartitionSpec as P

NS_STEPS = 2


NS_FIRST = 3.4445
NS_SECOND = -4.775
NS_THIRD = 2.0315
epsilon = 1e-06


def product(left, right):
    return jnp.dot(left, right, preferred_element_type=jnp.float32)


def product_bt(left, right):
    return lax.dot_general(
        left, right, (((1,), (1,)), ((), ())), preferred_element_type=jnp.float32
    )


def product_at(left, right):
    return lax.dot_general(
        left, right, (((0,), (0,)), ((), ())), preferred_element_type=jnp.float32
    )


def silu_parts(inputs):
    sigmoid_part = jax.nn.sigmoid(inputs)
    activation = inputs * sigmoid_part
    slopes = sigmoid_part * (1.0 + inputs * (1.0 - sigmoid_part))
    curves = sigmoid_part * (1.0 - sigmoid_part) * (2.0 + inputs * (1.0 - 2.0 * sigmoid_part))
    return (activation, slopes, curves)


def key_gradients(key_rows, value_rows, token_rates, gate_half, up_half, down_half):
    key_gate = product_bt(key_rows, gate_half)
    key_up = product_bt(key_rows, up_half)
    activation, slopes, curves = silu_parts(key_gate)
    key_act = (activation * key_up).astype(jnp.bfloat16)
    scaled = (token_rates[:, None] * value_rows.astype(jnp.float32)).astype(jnp.bfloat16)
    key_back = product_bt(scaled, down_half)
    gate_tok = (key_back * key_up * slopes).astype(jnp.bfloat16)
    up_tok = (key_back * activation).astype(jnp.bfloat16)
    partial_grads = (
        product_at(gate_tok, key_rows),
        product_at(up_tok, key_rows),
        product_at(key_act, scaled),
    )
    saved = (key_up, activation, slopes, curves, key_act, scaled, key_back, gate_tok, up_tok)
    return (partial_grads, saved)


def orthogonalize(moment):
    norm_value = jnp.sqrt(jnp.sum(moment * moment) + epsilon)
    current = (moment / norm_value).astype(jnp.bfloat16)
    records = []
    for number in range(NS_STEPS):
        gram_matrix = product_at(current, current).astype(jnp.bfloat16)
        poly_matrix = (
            NS_SECOND * gram_matrix.astype(jnp.float32)
            + NS_THIRD * product(gram_matrix, gram_matrix)
        ).astype(jnp.bfloat16)
        records.append((current, gram_matrix, poly_matrix))
        current = (NS_FIRST * current.astype(jnp.float32) + product(current, poly_matrix)).astype(
            jnp.bfloat16
        )
    return (current, (moment, norm_value, records))


def orthogonal_backward(record, cotangent):
    moment, norm_value, records = record
    upstream = cotangent
    for current, gram_matrix, poly_matrix in reversed(records):
        upstream_half = upstream.astype(jnp.bfloat16)
        poly_cot = product_at(current, upstream_half)
        poly_cot_half = poly_cot.astype(jnp.bfloat16)
        gram_cot = NS_SECOND * poly_cot + NS_THIRD * (
            product(poly_cot_half, gram_matrix) + product(gram_matrix, poly_cot_half)
        )
        sym_half = (gram_cot + gram_cot.T).astype(jnp.bfloat16)
        upstream = (
            NS_FIRST * upstream
            + product_bt(upstream_half, poly_matrix)
            + product(current, sym_half)
        )
    return upstream / norm_value - moment * (jnp.sum(upstream * moment) / norm_value**3)


def query_gradients(query_rows, output_cot, gate_half, up_half, down_half):
    query_gate = product_bt(query_rows, gate_half)
    query_up = product_bt(query_rows, up_half)
    activation, slopes, curves = silu_parts(query_gate)
    query_act = (activation * query_up).astype(jnp.bfloat16)
    query_back = product_bt(output_cot, down_half)
    gate_tok = (query_back * query_up * slopes).astype(jnp.bfloat16)
    up_tok = (query_back * activation).astype(jnp.bfloat16)
    queries_grad = (product(gate_tok, gate_half) + product(up_tok, up_half)).astype(jnp.bfloat16)
    partial_cots = (
        product_at(gate_tok, query_rows),
        product_at(up_tok, query_rows),
        product_at(query_act, output_cot),
    )
    return (queries_grad, partial_cots)


def key_backward(key_rows, value_rows, token_rates, saved, moments, gate_half, up_half, down_half):
    key_up, activation, slopes, curves, key_act, scaled, key_back, gate_tok, up_tok = saved
    mgate_half = moments[0].astype(jnp.bfloat16)
    mup_half = moments[1].astype(jnp.bfloat16)
    mdown_half = moments[2].astype(jnp.bfloat16)
    back_gate = product_bt(key_rows, mgate_half)
    back_up = product_bt(key_rows, mup_half)
    back_act = product_bt(scaled, mdown_half)
    back_keyback = (back_gate * key_up * slopes + back_up * activation).astype(jnp.bfloat16)
    back_keygate = (
        (back_up * key_back + back_act * key_up) * slopes + back_gate * key_back * key_up * curves
    ).astype(jnp.bfloat16)
    back_keyup = (back_gate * key_back * slopes + back_act * activation).astype(jnp.bfloat16)
    keys_grad = (
        product(gate_tok, mgate_half)
        + product(up_tok, mup_half)
        + product(back_keygate, gate_half)
        + product(back_keyup, up_half)
    ).astype(jnp.bfloat16)
    values_back = product(key_act, mdown_half) + product(back_keyback, down_half)
    values_grad = (token_rates[:, None] * values_back).astype(jnp.bfloat16)
    rates_grad = jnp.sum(value_rows.astype(jnp.float32) * values_back, axis=1)
    return (keys_grad, values_grad, rates_grad)


def on_device(query_rows, key_rows, value_rows, token_rates, output_cot, w_gate, w_up, w_down):
    gate_half = w_gate.astype(jnp.bfloat16)
    up_half = w_up.astype(jnp.bfloat16)
    down_half = w_down.astype(jnp.bfloat16)
    partial_grads, saved = key_gradients(
        key_rows, value_rows, token_rates, gate_half, up_half, down_half
    )
    totals = lax.psum((partial_grads[0], partial_grads[1], partial_grads[2]), ("view", "tok"))
    results = [orthogonalize(matrix) for matrix in totals]
    orthos = [entry[0].astype(jnp.float32) for entry in results]
    new_gate = (w_gate + orthos[0]).astype(jnp.bfloat16)
    new_up = (w_up + orthos[1]).astype(jnp.bfloat16)
    new_down = (w_down + orthos[2]).astype(jnp.bfloat16)
    queries_grad, partial_cots = query_gradients(query_rows, output_cot, new_gate, new_up, new_down)
    cot_totals = lax.psum((partial_cots[0], partial_cots[1], partial_cots[2]), ("view", "tok"))
    moments = [orthogonal_backward(results[index][1], cot_totals[index]) for index in range(3)]
    keys_grad, values_grad, rates_grad = key_backward(
        key_rows, value_rows, token_rates, saved, moments, gate_half, up_half, down_half
    )
    return (queries_grad, keys_grad, values_grad, rates_grad)


def solution(mesh):
    in_specs = (
        P(("group", "view", "tok"), None),
        P(("group", "view", "tok"), None),
        P(("group", "view", "tok"), None),
        P(("group", "view", "tok")),
        P(("group", "view", "tok"), None),
        P(),
        P(),
        P(),
    )
    out_specs = (
        P(("group", "view", "tok"), None),
        P(("group", "view", "tok"), None),
        P(("group", "view", "tok"), None),
        P(("group", "view", "tok")),
    )
    return jax.shard_map(
        on_device, mesh=mesh, in_specs=in_specs, out_specs=out_specs, check_vma=False
    )
```

profile of v0, /device:TPU:0, one launch (start us, length us, event | category | flops | bytes accessed | tf_op | source)
XLA Modules:
  0.0 336.9 jit_solution(8173933572449892007)
XLA Ops:
  7.2 0.9 copy-done
  8.1 1.7 fusion.95
  10.2 0.7 copy-done.62
  10.9 0.5 copy-done.72
  11.5 1.4 multiply_convert_fusion.4
  12.9 1.5 fusion.131
  14.4 1.5 fusion.123
  15.9 1.4 fusion.130
  17.6 109.4 %all-reduce.7.cloned.1.call-done = (f32[768,384]{1,0:T(8,128)}, f32[768,384]{1,0:T(8,128)}, f32[768,384]{1,0:T(8,128)}) async-done(((f32[768,384]{1,0:T(8,128)}, f32[768,384]{1,0:T(8,128)}, f32[768,384]{1,0:T(8,128)}), (f32[768,384]{1,0:T(8,128)}, f32[768,384]{1,0:T(8,128)}, f32[768,384]{1,0:T(8,128)})) %all-reduce.7.cloned.1.call-update) | async-done | bytes 3538960 | tf_op jit(solution)/shard_map/psum | solution.py:142
  127.0 2.3 multiply_reduce_fusion.3
  130.9 0.7 copy-done.66
  131.6 0.5 fusion.4
  132.7 0.7 copy-done.50
  133.8 1.4 fusion.8
  135.2 0.9 multiply_reduce_fusion.4
  137.7 0.7 copy-done.64
  138.5 0.5 fusion.2
  139.5 0.7 copy-done.46
  140.6 0.5 fusion.11
  141.8 1.3 convolution_bitcast_fusion.2
  143.1 1.3 convolution_bitcast_fusion.3
  144.4 0.9 multiply_reduce_fusion.5
  146.6 0.7 copy-done.44
  147.7 0.7 copy-done.68
  148.4 0.5 fusion
  149.5 0.7 copy-done.53
  150.2 1.1 fusion.34
  151.2 1.5 fusion.60
  152.8 4.1 %multiply_convert_fusion.1 = (bf16[256,768]{1,0:T(8,128)(2,1)}, bf16[256,768]{1,0:T(8,128)(2,1)}) fusion(f32[256,768]{1,0:T(8,128)} %convolution_bitcast_fusion.2, f32[256,768]{1,0:T(8,128)} %convolution_bitcast_fusion.3, bf16[256,384]{1,0:T(8,128)(2,1)S(1)} %copy-done.74, f32[768,384]{1,0:T(8,128)} %param.15, bf16[768,384]{1,0:T(8,128)(2,1)} %copy-done.30, ...), kind=kOutput, calls=%fused_computation.112 | convolution fusion | flops 382107648 | bytes 4620288 | tf_op jit(solution)/shard_map/dot_general | solution.py:20
  156.8 2.5 fusion.133
  159.3 1.5 fusion.135
  160.9 1.6 fusion.132
  162.5 1.0 fusion.41
  163.5 102.9 %all-reduce.5.cloned.1.call-done = (f32[768,384]{1,0:T(8,128)}, f32[768,384]{1,0:T(8,128)}, f32[768,384]{1,0:T(8,128)}) async-done(((f32[768,384]{1,0:T(8,128)}, f32[768,384]{1,0:T(8,128)}, f32[768,384]{1,0:T(8,128)}), (f32[768,384]{1,0:T(8,128)}, f32[768,384]{1,0:T(8,128)}, f32[768,384]{1,0:T(8,128)})) %all-reduce.5.cloned.1.call-update) | async-done | bytes 3538960 | tf_op jit(solution)/shard_map/psum | solution.py:149
  266.4 3.5 %convolution_add_fusion.11 = f32[768,384]{1,0:T(8,128)} fusion(bf16[384,384]{1,0:T(8,128)(2,1)} %copy-done.52, f32[768,384]{1,0:T(8,128)} %get-tuple-element.4), kind=kOutput, calls=%fused_computation.11 | convolution fusion | flops 227377152 | bytes 2654208 | tf_op jit(solution)/shard_map/dot_general | solution.py:20
  271.6 1.1 copy.15
  272.7 2.2 convolution_add_fusion.10
  274.9 1.8 convolution_add_fusion.9
  276.7 1.3 fusion.82
  278.0 1.5 convolution_add_fusion.3
  281.2 1.1 copy.20
  282.3 2.2 convolution_add_fusion.2
  284.5 1.5 convolution_add_fusion.1
  286.1 1.3 fusion.70
  287.4 1.6 convolution_add_fusion.7
  290.6 1.1 copy.17
  291.7 2.2 convolution_add_fusion.6
  293.9 1.5 convolution_add_fusion.5
  295.5 1.3 fusion.76
  297.5 1.1 copy.16
  298.6 3.8 %multiply_reduce_fusion.2 = (f32[]{:T(128)}, f32[768,384]{1,0:T(8,128)}) fusion(f32[768,384]{1,0:T(8,128)S(1)} %copy-done.1, f32[768,384]{1,0:T(8,128)} %convolution_add_fusion.9, bf16[768,384]{1,0:T(8,128)(2,1)} %copy-done.11, f32[384,384]{1,0:T(8,128)S(1)} %fusion.24, f32[384,384]{0,1:T(8,128)} %copy.16), kind=kOutput, calls=%fused_computation.90 | convolution fusion | flops 227672064 | bytes 5308420 | tf_op jit(solution)/shard_map/dot_general | solution.py:16
  303.1 1.5 subtract_convert_fusion.2
  304.9 1.3 convolution_bitcast_fusion
  307.0 1.1 copy.21
  308.0 1.4 fusion.104
  309.8 1.1 copy.18
  310.9 4.0 %multiply_reduce_fusion = (f32[]{:T(128)}, f32[768,384]{1,0:T(8,128)}) fusion(f32[768,384]{1,0:T(8,128)S(1)} %copy-done.2, f32[768,384]{1,0:T(8,128)} %convolution_add_fusion.1, bf16[768,384]{1,0:T(8,128)(2,1)} %copy-done.9, f32[384,384]{1,0:T(8,128)} %copy-done.6, f32[384,384]{0,1:T(8,128)} %copy.21), kind=kOutput, calls=%fused_computation.86 | convolution fusion | flops 227672064 | bytes 5308420 | tf_op jit(solution)/shard_map/dot_general | solution.py:16
  315.6 3.8 %multiply_reduce_fusion.1 = (f32[]{:T(128)}, f32[768,384]{1,0:T(8,128)}) fusion(f32[768,384]{1,0:T(8,128)S(1)} %copy-done.4, f32[768,384]{1,0:T(8,128)} %convolution_add_fusion.5, bf16[768,384]{1,0:T(8,128)(2,1)} %copy-done.7, f32[384,384]{1,0:T(8,128)S(1)} %fusion.20, f32[384,384]{0,1:T(8,128)} %copy.18), kind=kOutput, calls=%fused_computation.88 | convolution fusion | flops 227672064 | bytes 5308420 | tf_op jit(solution)/shard_map/dot_general | solution.py:16
  320.0 2.0 subtract_convert_fusion
  322.5 0.6 copy-done.39
  323.0 0.6 fusion.136
  325.6 0.8 convolution_add_fusion.26
  326.9 1.3 fusion.42
  328.1 1.9 fusion.59
  (178 shorter events, 16.3 us)
Async XLA Ops:
  7.2 2.6 copy-start.23
  7.2 119.8 %all-reduce.7.cloned.1.call-start = ((), (), s32[]{:S(2)}) async-start(), calls=%async_computation.1 | async-start | bytes 7077888 | tf_op jit(solution)/shard_map/psum | solution.py:142
  9.8 3.1 copy-start.55
  9.8 1.1 copy-start.62
  9.8 1.1 copy-start.71
  9.8 1.6 copy-start.72
  11.5 1.5 copy-start.57
  12.9 3.0 copy-start.34
  12.9 3.0 copy-start.38
  12.9 3.0 copy-start.32
  17.4 249.1 %all-reduce.5.cloned.1.call-start = ((), (), s32[]{:S(2)}) async-start(), calls=%async_computation | async-start | bytes 7077888 | tf_op jit(solution)/shard_map/psum | solution.py:149
  127.0 3.0 copy-start.1
  130.6 1.6 copy-start.42
  132.2 1.6 copy-start.15
  132.2 1.6 copy-start.21
  133.8 1.4 copy-start.52
  133.8 1.4 copy-start.3
  137.4 1.6 copy-start.40
  139.0 1.6 copy-start.13
  139.0 1.6 copy-start.24
  140.6 1.2 copy-start.5
  140.6 1.2 copy-start.29
  143.1 1.3 copy-start.2
  146.1 1.6 copy-start.9
  148.9 2.3 copy-start.30
  148.9 2.3 copy-start.60
  148.9 2.3 copy-start.61
  149.0 2.3 copy-start.74
  156.8 2.5 copy-start.36
  160.8 1.6 copy-start.37
  266.4 3.5 %copy-start.16 = (bf16[768,384]{1,0:T(8,128)(2,1)S(1)}, bf16[768,384]{1,0:T(8,128)(2,1)}, u32[]{:S(2)}) copy-start(bf16[768,384]{1,0:T(8,128)(2,1)} %copy-done.15) | copy-start | bytes 1769476
  266.4 3.5 %copy-start.28 = (f32[768,384]{1,0:T(8,128)S(1)}, f32[768,384]{1,0:T(8,128)}, u32[]{:S(2)}) copy-start(f32[768,384]{1,0:T(8,128)} %get-tuple-element.4) | copy-start | bytes 3538948
  272.7 2.2 copy-start.67
  274.9 1.8 copy-start.12
  276.7 1.3 copy-start.27
  276.7 1.3 copy-start.70
  278.0 1.6 copy-start.31
  282.3 2.2 copy-start.69
  284.5 1.6 copy-start.10
  286.1 1.3 copy-start.26
  286.1 1.3 copy-start.49
  287.4 1.6 copy-start.14
  291.7 2.2 copy-start.65
  293.9 1.6 copy-start.8
  295.5 1.3 copy-start.18
  295.5 1.3 copy-start.43
  303.1 1.5 copy-start.35
  304.6 1.7 copy-start.17
  304.6 1.7 copy-start.45
  306.6 1.5 copy-start.19
  306.9 2.5 copy-start.6
  307.0 2.5 copy-start.20
  308.0 1.4 copy-start.41
  310.9 4.7 %copy-start.4 = (f32[768,384]{1,0:T(8,128)S(1)}, f32[768,384]{1,0:T(8,128)}, u32[]{:S(2)}) copy-start(f32[768,384]{1,0:T(8,128)} %get-tuple-element.9) | copy-start | bytes 3538948
  320.0 2.0 copy-start.63
  322.0 1.0 copy-start.39
  323.0 1.1 copy-start.33
  323.0 1.5 copy-start.59
  323.0 1.5 copy-start.75
  323.7 1.3 copy-start.56
  323.7 1.5 copy-start.58
  324.1 1.5 copy-start.22
  325.6 1.3 copy-start.25
  326.9 1.3 copy-start.73
  (14 other events, 11.3 us)
Sparse Core Ops, SparseCore 0:
  17.5 109.4 all-reduce.6
  161.0 105.4 all-reduce.4
where the time goes:
time: 338 us; the launch traced here: 337 us
  waiting for transfers between devices  212 us (63%)
  matrix products  79.5 us (24%)
  between operations  19.1 us (6%)
  local copies, waits for them, and re-layouts  17.9 us (5%)
  other arithmetic  7.84 us (2%)
    psum x1, waiting for transfers between devices, on_device(): lax.psum((partial_grads[0], partial_grads[1], partial_grads[2]), ('view',...  109 us
    psum x1, waiting for transfers between devices, on_device(): lax.psum((partial_cots[0], partial_cots[1], partial_cots[2]), ('view', 't...  103 us
    dot_general x37, matrix products, product(): return jnp.dot(left, right, preferred_element_type=jnp.float32)  37.5 us
    dot_general x15, matrix products, product_bt(): lax.dot_general(left, right, (((1,), (1,)), ((), ())), preferred_element_...  23.7 us
    dot_general x18, matrix products, product_at(): lax.dot_general(left, right, (((0,), (0,)), ((), ())), preferred_element_...  18.3 us
    unnamed x152, local copies, waits for them, and re-layouts  11.5 us
  transfers between devices with their start and end apart: 2, of which 2 were waited for; matrix products, arithmetic and copies ran while one was open for 1% of the time, Pallas kernels for 0%

commit v1 on v0

v1 whole, which is shorter than its diff:
```python
import functools

import jax
import jax.numpy as jnp
from jax import lax
from jax.experimental import pallas as pl
from jax.experimental.pallas import tpu as pltpu
from jax.sharding import PartitionSpec as P

NS_STEPS = 2
NS_FIRST = 3.4445
NS_SECOND = -4.775
NS_THIRD = 2.0315
EPSILON = 1e-06
MESH = pl.DeviceIdType.MESH
BF = jnp.bfloat16
F32 = jnp.float32
GATE, UP, DOWN = 0, 1, 2
HALVINGS = 3


def dot(left, right):
    return jnp.dot(left, right, preferred_element_type=F32)


def dot_bt(left, right):
    return lax.dot_general(left, right, (((1,), (1,)), ((), ())), preferred_element_type=F32)


def total_of(values):
    return jnp.sum(jnp.sum(values, axis=1, keepdims=True), axis=0, keepdims=True)


def bits_of(axis, size):
    bits, bit = [], 1
    while bit < size:
        bits.append((axis, bit))
        bit *= 2
    return bits


class Summing:
    def __init__(self, orders, acc, res, halved, exchanged, between, send_sem, recv_sem, number, matrix, half):
        self.order = orders[half]
        self.where = (number, matrix, half)
        self.acc, self.res = acc.at[number, matrix, half], res.at[number, matrix, half]
        self.halved = [ref.at[number, matrix, half] for ref in halved]
        self.exchanged = [ref.at[number, matrix, half] for ref in exchanged]
        self.between = [ref.at[number, matrix, half] for ref in between]
        self.send_sem, self.recv_sem = send_sem, recv_sem
        self.extent = acc.shape[-2]
        self.offset, self.size = 0, self.extent
        self.levels = len(self.order)
        self.halvings = min(HALVINGS, self.levels - 1)
        self.offsets = []
        self.step = 0
        self.pending, self.sent = None, []

    def side(self, level):
        axis, bit = self.order[level]
        place = lax.axis_index(axis)
        mine = lax.rem(place // bit, 2)
        return mine, {axis: place + bit * (1 - 2 * mine)}

    def rows(self, offset, size):
        if isinstance(offset, int):
            return pl.ds(offset, size)
        return pl.ds(pl.multiple_of(offset, 16), size)

    def send(self, source, target, device):
        slot = self.where + (self.step,)
        copy = pltpu.make_async_remote_copy(
            src_ref=source,
            dst_ref=target,
            send_sem=self.send_sem.at[slot],
            recv_sem=self.recv_sem.at[slot],
            device_id=device,
            device_id_type=MESH,
        )
        copy.start()
        self.pending = copy
        self.sent.append(copy)

    def advance(self):
        step, halvings, levels = self.step, self.halvings, self.levels
        if step > 0:
            self.pending.wait_recv()
            last = step - 1
            if last < halvings:
                here = self.rows(self.offset, self.size)
                self.acc[here, :] = (
                    self.acc[here, :].astype(F32) + self.halved[last][...].astype(F32)
                ).astype(BF)
            elif last < levels:
                place = last - halvings
                if place == 0:
                    own = self.acc[self.rows(self.offset, self.size), :]
                else:
                    own = self.between[place - 1][...]
                summed = (own.astype(F32) + self.exchanged[place][...].astype(F32)).astype(BF)
                if last == levels - 1:
                    self.res[self.rows(self.offset, self.size), :] = summed
                else:
                    self.between[place][...] = summed
            else:
                back = halvings - 1 - (last - levels)
                self.offset, self.size = self.offsets[back], self.size * 2
        if step < halvings:
            mine, device = self.side(step)
            size = self.size // 2
            self.offsets.append(self.offset)
            self.send(self.acc.at[self.rows(self.offset + (1 - mine) * size, size), :], self.halved[step], device)
            self.offset, self.size = self.offset + mine * size, size
        elif step < levels:
            place = step - halvings
            _, device = self.side(step)
            source = self.acc.at[self.rows(self.offset, self.size), :] if place == 0 else self.between[place - 1]
            self.send(source, self.exchanged[place], device)
        elif step < levels + halvings:
            _, device = self.side(halvings - 1 - (step - levels))
            here = self.rows(self.offset, self.size)
            self.send(self.res.at[here, :], self.res.at[here, :], device)
        self.step += 1

    @property
    def steps(self):
        return self.levels + self.halvings


def kernel(
    orders, n_halved, n_exchanged,
    q_ref, k_ref, v_ref, r_ref, o_ref, wg_ref, wu_ref, wd_ref,
    dq_ref, dk_ref, dv_ref, dr_ref,
    acc, res, xs, grams, polys, new_t, w_t, saved, toks, send_sem, recv_sem, *levels,
):
    halved, exchanged = levels[:n_halved], levels[n_halved:n_halved + n_exchanged]
    between = levels[n_halved + n_exchanged:]
    width = acc.shape[-1]
    halves = new_t.shape[-1] // width

    barrier = pltpu.get_barrier_semaphore()
    for axis, bit in orders[0]:
        place = lax.axis_index(axis)
        peer = place + bit * (1 - 2 * lax.rem(place // bit, 2))
        pl.semaphore_signal(barrier, inc=1, device_id={axis: peer}, device_id_type=MESH)

    chunks = {}
    every = []

    def begin(number, matrix, values):
        for half in range(halves):
            acc[number, matrix, half] = values[:, half * width:(half + 1) * width].astype(BF)
            chunk = Summing(
                orders, acc, res, halved, exchanged, between, send_sem, recv_sem, number, matrix, half
            )
            chunk.advance()
            chunks[number, matrix, half] = chunk
            every.append(chunk)

    def pump(number, matrix):
        for half in range(halves):
            chunk = chunks[number, matrix, half]
            if chunk.step <= chunk.steps:
                chunk.advance()

    def total(number, matrix):
        return jnp.concatenate([res[number, matrix, half] for half in range(halves)], axis=1)

    k = k_ref[...]
    k_t = k.T
    key_gate = dot_bt(k, wg_ref[...].astype(BF))
    key_up = dot_bt(k, wu_ref[...].astype(BF))
    sig = jax.nn.sigmoid(key_gate)
    act = key_gate * sig
    slopes = sig * (1.0 + key_gate * (1.0 - sig))
    toks[DOWN] = (act * key_up).astype(BF)
    scaled = (r_ref[...] * v_ref[...].astype(F32)).astype(BF)
    down_grad = dot(scaled.T, toks[DOWN])
    pl.semaphore_wait(barrier, len(orders[0]))
    begin(0, DOWN, down_grad)
    key_back = dot_bt(scaled, wd_ref[...].astype(BF))
    toks[UP] = (key_back * act).astype(BF)
    begin(0, UP, dot(k_t, toks[UP]))
    toks[GATE] = (key_back * key_up * slopes).astype(BF)
    begin(0, GATE, dot(k_t, toks[GATE]))
    pump(0, DOWN)
    curves = sig * (1.0 - sig) * (2.0 + key_gate * (1.0 - 2.0 * sig))
    saved[0] = act
    saved[1] = key_up * slopes
    pump(0, UP)
    pump(0, DOWN)
    saved[2] = key_back * slopes
    saved[3] = key_back * key_up * curves
    pump(0, GATE)
    pump(0, UP)
    pump(0, DOWN)
    w_t[DOWN] = wd_ref[...].T
    pump(0, GATE)
    pump(0, UP)
    pump(0, DOWN)
    w_t[UP] = wu_ref[...].T
    pump(0, GATE)
    pump(0, UP)
    pump(0, DOWN)
    w_t[GATE] = wg_ref[...].T

    inverse = {}

    def ortho_start(matrix):
        moment = total(0, matrix).astype(F32)
        inverse[matrix] = 1.0 / jnp.sqrt(total_of(moment * moment) + EPSILON)
        xs[matrix, 0] = (moment * inverse[matrix]).astype(BF)

    def ortho_step(matrix, number):
        current = xs[matrix, number]
        gram = dot_bt(current, current).astype(BF)
        poly = (NS_SECOND * gram.astype(F32) + NS_THIRD * dot(gram, gram)).astype(BF)
        grams[matrix, number] = gram
        polys[matrix, number] = poly
        following = (NS_FIRST * current.astype(F32) + dot(poly, current)).astype(BF)
        if number + 1 < NS_STEPS:
            xs[matrix, number + 1] = following
        else:
            new_t[matrix] = (w_t[matrix] + following.astype(F32)).astype(BF)

    def ortho(matrix, others):
        ortho_start(matrix)
        for number in range(NS_STEPS):
            for other in others:
                pump(0, other)
            ortho_step(matrix, number)

    def finish(number, matrix):
        while chunks[number, matrix, 0].step <= chunks[number, matrix, 0].steps:
            pump(number, matrix)

    pump(0, GATE)
    pump(0, UP)
    pump(0, DOWN)
    pump(0, GATE)
    pump(0, UP)
    finish(0, DOWN)
    pump(0, GATE)
    pump(0, UP)
    ortho(DOWN, (GATE, UP))
    finish(0, UP)
    query_back = dot(o_ref[...], new_t[DOWN])
    ortho(UP, (GATE,))
    finish(0, GATE)
    q = q_ref[...]
    query_up = dot(q, new_t[UP])
    q_t = q.T
    o_t = o_ref[...].T
    ortho(GATE, ())

    query_gate = dot(q, new_t[GATE])
    sig = jax.nn.sigmoid(query_gate)
    act = query_gate * sig
    slopes = sig * (1.0 + query_gate * (1.0 - sig))
    begin(1, DOWN, dot(o_t, (act * query_up).astype(BF)))
    qup_tok = (query_back * act).astype(BF)
    begin(1, UP, dot(q_t, qup_tok))
    qgate_tok = (query_back * query_up * slopes).astype(BF)
    begin(1, GATE, dot(q_t, qgate_tok))
    pump(1, DOWN)
    pump(1, UP)
    queries = dot_bt(qup_tok, new_t[UP])
    pump(1, DOWN)
    pump(1, GATE)
    pump(1, UP)
    pump(1, DOWN)
    dq_ref[...] = (queries + dot_bt(qgate_tok, new_t[GATE])).astype(BF)
    for _ in range(3):
        pump(1, GATE)
        pump(1, UP)
        pump(1, DOWN)

    def unortho(matrix, others):
        upstream_half = total(1, matrix)
        upstream = upstream_half.astype(F32)
        for number in reversed(range(NS_STEPS)):
            for other in others:
                pump(1, other)
            current = xs[matrix, number]
            poly_cot = dot_bt(current, upstream_half)
            poly_cot = poly_cot + poly_cot.T
            mixed = dot(poly_cot.astype(BF), grams[matrix, number])
            sym = (NS_SECOND * poly_cot + NS_THIRD * (mixed + mixed.T)).astype(BF)
            upstream = NS_FIRST * upstream + dot(
                jnp.concatenate([polys[matrix, number], sym], axis=1),
                jnp.concatenate([upstream_half, current], axis=0),
            )
            upstream_half = upstream.astype(BF)
        moment = total(0, matrix).astype(F32)
        inv = inverse[matrix]
        return (upstream * inv - moment * (total_of(upstream * moment) * (inv * inv * inv))).astype(BF)

    pump(1, GATE)
    pump(1, UP)
    finish(1, DOWN)
    mdown = unortho(DOWN, (GATE, UP))
    finish(1, UP)
    scaled = (r_ref[...] * v_ref[...].astype(F32)).astype(BF)
    back_act = dot(scaled, mdown)
    values = dot_bt(toks[DOWN], mdown)
    mup = unortho(UP, (GATE,))
    finish(1, GATE)
    k = k_ref[...]
    back_up = dot(k, mup)
    keys = dot_bt(toks[UP], mup)
    mgate = unortho(GATE, ())
    back_gate = dot(k, mgate)
    back_keyback = (back_gate * saved[1] + back_up * saved[0]).astype(BF)
    values = values + dot(back_keyback, wd_ref[...].astype(BF))
    dv_ref[...] = (r_ref[...] * values).astype(BF)
    dr_ref[...] = jnp.sum(v_ref[...].astype(F32) * values, axis=1, keepdims=True)
    back_keygate = (back_up * saved[2] + back_act * saved[1] + back_gate * saved[3]).astype(BF)
    back_keyup = (back_gate * saved[2] + back_act * saved[0]).astype(BF)
    keys = keys + dot_bt(toks[GATE], mgate)
    keys = keys + dot(back_keygate, wg_ref[...].astype(BF)) + dot(back_keyup, wu_ref[...].astype(BF))
    dk_ref[...] = keys.astype(BF)
    for chunk in every:
        for copy in chunk.sent:
            copy.wait_send()


def on_device(n_view, n_tok, q, k, v, r, o, wg, wu, wd):
    rows, features = q.shape
    hidden = wg.shape[0]
    tok_bits, view_bits = bits_of("tok", n_tok), bits_of("view", n_view)
    orders = (tok_bits + view_bits, tok_bits[:1] + view_bits + tok_bits[1:])
    levels = len(orders[0])
    n_halved = min(HALVINGS, levels - 1)
    n_exchanged = levels - n_halved
    width = hidden // 2
    segment = features >> n_halved
    lead = (2, 3, 2)
    vmem = pl.BlockSpec(memory_space=pltpu.VMEM)
    steps = levels + n_halved
    outs = pl.pallas_call(
        functools.partial(kernel, orders, n_halved, n_exchanged),
        out_shape=(
            jax.ShapeDtypeStruct((rows, features), BF),
            jax.ShapeDtypeStruct((rows, features), BF),
            jax.ShapeDtypeStruct((rows, features), BF),
            jax.ShapeDtypeStruct((rows, 1), F32),
        ),
        in_specs=[vmem] * 8,
        out_specs=(vmem,) * 4,
        scratch_shapes=[
            pltpu.VMEM(lead + (features, width), BF),
            pltpu.VMEM(lead + (features, width), BF),
            pltpu.VMEM((3, NS_STEPS, features, hidden), BF),
            pltpu.VMEM((3, NS_STEPS, features, features), BF),
            pltpu.VMEM((3, NS_STEPS, features, features), BF),
            pltpu.VMEM((3, features, hidden), BF),
            pltpu.VMEM((3, features, hidden), F32),
            pltpu.VMEM((4, rows, hidden), F32),
            pltpu.VMEM((3, rows, hidden), BF),
            pltpu.SemaphoreType.DMA(lead + (steps,)),
            pltpu.SemaphoreType.DMA(lead + (steps,)),
        ]
        + [pltpu.VMEM(lead + (features >> (level + 1), width), BF) for level in range(n_halved)]
        + [pltpu.VMEM(lead + (segment, width), BF) for _ in range(n_exchanged)]
        + [pltpu.VMEM(lead + (segment, width), BF) for _ in range(n_exchanged - 1)],
        compiler_params=pltpu.CompilerParams(
            collective_id=0, has_side_effects=True, vmem_limit_bytes=60 * 1024 * 1024
        ),
    )(q, k, v, r.reshape(rows, 1), o, wg, wu, wd)
    return (outs[0], outs[1], outs[2], outs[3].reshape(rows))


def solution(mesh):
    rows = P(("group", "view", "tok"), None)
    flat = P(("group", "view", "tok"))
    return jax.shard_map(
        functools.partial(on_device, mesh.shape["view"], mesh.shape["tok"]),
        mesh=mesh,
        in_specs=(rows, rows, rows, flat, rows, P(), P(), P()),
        out_specs=(rows, rows, rows, flat),
        check_vma=False,
    )
```

time: 338 us -> 93.6 us (0.28)
  waiting for transfers between devices: 212 us -> 0 us
  Pallas kernels: 0 us -> 84.8 us
  matrix products: 79.5 us -> 0 us
  between operations: 19.1 us -> 0.64 us
  local copies, waits for them, and re-layouts: 17.9 us -> 6.34 us
  other arithmetic: 7.84 us -> 1.58 us
    psum x2 -> x0, waiting for transfers between devices: 212 us -> none  [the longest x1 109 us: on_device(): lax.psum((partial_grads[0], partial_grads[1], partial_grads[2]), ('view',...]
    pallas_call x0 -> x1, Pallas kernels: none -> 84.8 us  [on_device(): pl.pallas_call(functools.partial(kernel, orders, n_halved, n_exchanged),...]
    dot_general x70 -> x0, matrix products: 79.5 us -> none  [the longest x37 37.5 us: product(): return jnp.dot(left, right, preferred_element_type=jnp.float32)]
    unnamed x152 -> x3, local copies, waits for them, and re-layouts: 11.5 us -> 4.87 us
    add x6 -> x0, local copies, waits for them, and re-layouts: 6.4 us -> none  [orthogonal_backward(): NS_SECOND * poly_cot]
    reduce_sum x3 -> x0, other arithmetic: 4.07 us -> none  [orthogonalize(): norm_value = jnp.sqrt(jnp.sum(moment * moment) + epsilon)]
    convert_element_type x5 -> x0, other arithmetic: 3.76 us -> none  [the longest x1 2.01 us: key_backward(): mdown_half = moments[2].astype(jnp.bfloat16)]
  transfers between devices with their start and end apart: 2 -> 0, of which waited for: 2 -> 0; matrix products, arithmetic and copies ran while one was open for 1% -> 0% of each run, Pallas kernels for 0% -> 0%
where the time goes in v1:
time: 93.6 us; the launch traced here: 93.4 us
  Pallas kernels  84.8 us (91%)
  local copies, waits for them, and re-layouts  6.34 us (7%)
  other arithmetic  1.58 us (2%)
    pallas_call x1, Pallas kernels, on_device(): pl.pallas_call(functools.partial(kernel, orders, n_halved, n_exchanged),...  84.8 us
    unnamed x3, local copies, waits for them, and re-layouts  4.87 us

profile of v1, /device:TPU:0, one launch (start us, length us, event | category | flops | bytes accessed | tf_op | source)
XLA Modules:
  0.0 93.4 jit_solution(6921482170102203904)
XLA Ops:
  0.6 1.5 %copy.12.r_ref = f32[256,1]{1,0:T(8,128)} copy(f32[256,1]{0,1:T(1,128)} %bitcast.1) | data formatting | bytes 2048 | tf_op jit(solution)/shard_map/reshape | solution.py:369
  2.1 84.8 %shard_map.111 = (bf16[256,384]{1,0:T(8,128)(2,1)}, bf16[256,384]{1,0:T(8,128)(2,1)}, bf16[256,384]{1,0:T(8,128)(2,1)}, f32[256,1]{1,0:T(8,128)}) custom-call(bf16[256,384]{1,0:T(8,128)(2,1)} %q_ref.1, bf16[256,384]{1,0:T(8,128)(2,1)} %k_ref.1, bf16[256,384]{1,0:T(8,128)(2,1)} %v_ref.1, f32[256,1]{1,0:T(8,128)} %copy.12.r_ref, bf16[256,384]{1,0:T(8,128)(2,1)} %o_ref.1, ...), custom_call_target="tpu_custom_call" | custom-call | tf_op jit(solution)/shard_map/pallas_call | solution.py:340
  87.0 1.6 %reduce = f32[256]{0:T(256)} reduce(f32[256,1]{1,0:T(8,128)} %get-tuple-element.11, f32[]{:T(128)} %constant), dimensions={1}, to_apply=%get-tuple-element.11.reduce_sub_computation | reduce | bytes 2052 | tf_op jit(solution)/shard_map/pallas_call | solution.py:340
  88.5 1.6 %copy.16 = bf16[256,384]{1,0:T(8,128)(2,1)} copy(bf16[256,384]{1,0:T(8,128)(2,1)} %get-tuple-element.16) | data formatting | bytes 393216
  90.2 1.6 %copy.17 = bf16[256,384]{1,0:T(8,128)(2,1)} copy(bf16[256,384]{1,0:T(8,128)(2,1)} %get-tuple-element.17) | data formatting | bytes 393216
  91.8 1.6 %copy.18 = bf16[256,384]{1,0:T(8,128)(2,1)} copy(bf16[256,384]{1,0:T(8,128)(2,1)} %get-tuple-element.18) | data formatting | bytes 393216

commit v2 on v1

--- a/solution.py
+++ b/solution.py
@@ -163,9 +163,15 @@
             if chunk.step <= chunk.steps:
                 chunk.advance()
 
+    def finish(number, matrix):
+        while chunks[number, matrix, 0].step <= chunks[number, matrix, 0].steps:
+            pump(number, matrix)
+
     def total(number, matrix):
+        finish(number, matrix)
         return jnp.concatenate([res[number, matrix, half] for half in range(halves)], axis=1)
 
+    rates = jnp.broadcast_to(r_ref[...], (8, r_ref.shape[1])).T[:, :1]
     k = k_ref[...]
     k_t = k.T
     key_gate = dot_bt(k, wg_ref[...].astype(BF))
@@ -174,7 +180,7 @@
     act = key_gate * sig
     slopes = sig * (1.0 + key_gate * (1.0 - sig))
     toks[DOWN] = (act * key_up).astype(BF)
-    scaled = (r_ref[...] * v_ref[...].astype(F32)).astype(BF)
+    scaled = (rates * v_ref[...].astype(F32)).astype(BF)
     down_grad = dot(scaled.T, toks[DOWN])
     pl.semaphore_wait(barrier, len(orders[0]))
     begin(0, DOWN, down_grad)
@@ -223,64 +229,52 @@
         else:
             new_t[matrix] = (w_t[matrix] + following.astype(F32)).astype(BF)
 
-    def ortho(matrix, others):
+    def ortho(matrix):
         ortho_start(matrix)
         for number in range(NS_STEPS):
-            for other in others:
-                pump(0, other)
             ortho_step(matrix, number)
 
-    def finish(number, matrix):
-        while chunks[number, matrix, 0].step <= chunks[number, matrix, 0].steps:
+    def tick(number, *matrices):
+        for matrix in matrices:
             pump(number, matrix)
 
-    pump(0, GATE)
-    pump(0, UP)
-    pump(0, DOWN)
-    pump(0, GATE)
-    pump(0, UP)
-    finish(0, DOWN)
-    pump(0, GATE)
-    pump(0, UP)
-    ortho(DOWN, (GATE, UP))
-    finish(0, UP)
-    query_back = dot(o_ref[...], new_t[DOWN])
-    ortho(UP, (GATE,))
-    finish(0, GATE)
+    tick(0, GATE, UP, DOWN)
     q = q_ref[...]
-    query_up = dot(q, new_t[UP])
     q_t = q.T
     o_t = o_ref[...].T
-    ortho(GATE, ())
+    tick(0, GATE, UP, DOWN)
+    ortho(DOWN)
+    tick(0, GATE, UP)
+    query_back = dot(o_ref[...], new_t[DOWN])
+    ortho(UP)
+    tick(0, GATE)
+    query_up = dot(q, new_t[UP])
+    ortho(GATE)
 
     query_gate = dot(q, new_t[GATE])
     sig = jax.nn.sigmoid(query_gate)
     act = query_gate * sig
     slopes = sig * (1.0 + query_gate * (1.0 - sig))
     begin(1, DOWN, dot(o_t, (act * query_up).astype(BF)))
+    qgate_tok = (query_back * query_up * slopes).astype(BF)
+    begin(1, GATE, dot(q_t, qgate_tok))
+    tick(1, DOWN)
     qup_tok = (query_back * act).astype(BF)
     begin(1, UP, dot(q_t, qup_tok))
-    qgate_tok = (query_back * query_up * slopes).astype(BF)
-    begin(1, GATE, dot(q_t, qgate_tok))
-    pump(1, DOWN)
-    pump(1, UP)
+    tick(1, GATE, DOWN)
     queries = dot_bt(qup_tok, new_t[UP])
-    pump(1, DOWN)
-    pump(1, GATE)
-    pump(1, UP)
-    pump(1, DOWN)
+    tick(1, UP, GATE, DOWN)
     dq_ref[...] = (queries + dot_bt(qgate_tok, new_t[GATE])).astype(BF)
+    tick(1, UP, GATE, DOWN)
+    scaled = (rates * v_ref[...].astype(F32)).astype(BF)
+    k = k_ref[...]
     for _ in range(3):
-        pump(1, GATE)
-        pump(1, UP)
-        pump(1, DOWN)
-
-    def unortho(matrix, others):
+        tick(1, UP, GATE, DOWN)
+
+    def unortho(matrix):
         upstream_half = total(1, matrix)
         upstream = upstream_half.astype(F32)
         for number in reversed(range(NS_STEPS)):
-            for other in others:
-                pump(1, other)
             current = xs[matrix, number]
             poly_cot = dot_bt(current, upstream_half)
             poly_cot = poly_cot + poly_cot.T
@@ -295,40 +289,43 @@
         inv = inverse[matrix]
         return (upstream * inv - moment * (total_of(upstream * moment) * (inv * inv * inv))).astype(BF)
 
-    pump(1, GATE)
-    pump(1, UP)
-    finish(1, DOWN)
-    mdown = unortho(DOWN, (GATE, UP))
-    finish(1, UP)
-    scaled = (r_ref[...] * v_ref[...].astype(F32)).astype(BF)
+    mdown = unortho(DOWN)
+    tick(1, UP, GATE)
     back_act = dot(scaled, mdown)
     values = dot_bt(toks[DOWN], mdown)
-    mup = unortho(UP, (GATE,))
-    finish(1, GATE)
-    k = k_ref[...]
+    mgate = unortho(GATE)
+    tick(1, UP)
+    back_gate = dot(k, mgate)
+    keys = dot_bt(toks[GATE], mgate)
+    back_keyup = (back_gate * saved[2] + back_act * saved[0]).astype(BF)
+    keys = keys + dot(back_keyup, wu_ref[...].astype(BF))
+    keygate_part = back_act * saved[1] + back_gate * saved[3]
+    keyback_part = back_gate * saved[1]
+    mup = unortho(UP)
     back_up = dot(k, mup)
-    keys = dot_bt(toks[UP], mup)
-    mgate = unortho(GATE, ())
-    back_gate = dot(k, mgate)
-    back_keyback = (back_gate * saved[1] + back_up * saved[0]).astype(BF)
+    back_keyback = (keyback_part + back_up * saved[0]).astype(BF)
     values = values + dot(back_keyback, wd_ref[...].astype(BF))
-    dv_ref[...] = (r_ref[...] * values).astype(BF)
-    dr_ref[...] = jnp.sum(v_ref[...].astype(F32) * values, axis=1, keepdims=True)
-    back_keygate = (back_up * saved[2] + back_act * saved[1] + back_gate * saved[3]).astype(BF)
-    back_keyup = (back_gate * saved[2] + back_act * saved[0]).astype(BF)
-    keys = keys + dot_bt(toks[GATE], mgate)
-    keys = keys + dot(back_keygate, wg_ref[...].astype(BF)) + dot(back_keyup, wu_ref[...].astype(BF))
+    dv_ref[...] = (rates * values).astype(BF)
+    rates_grad = jnp.sum(v_ref[...].astype(F32) * values, axis=1, keepdims=True)
+    dr_ref[...] = jnp.broadcast_to(rates_grad, (rates_grad.shape[0], 128)).T[:1]
+    back_keygate = (keygate_part + back_up * saved[2]).astype(BF)
+    keys = keys + dot_bt(toks[UP], mup) + dot(back_keygate, wg_ref[...].astype(BF))
     dk_ref[...] = keys.astype(BF)
     for chunk in every:
         for copy in chunk.sent:
             copy.wait_send()
 
 
+def handing(*refs):
+    for source, target in zip(refs[:4], refs[4:]):
+        target[...] = source[...]
+
+
 def on_device(n_view, n_tok, q, k, v, r, o, wg, wu, wd):
     rows, features = q.shape
     hidden = wg.shape[0]
     tok_bits, view_bits = bits_of("tok", n_tok), bits_of("view", n_view)
-    orders = (tok_bits + view_bits, tok_bits[:1] + view_bits + tok_bits[1:])
+    orders = (tok_bits + view_bits, tok_bits[:1] + view_bits[:1] + tok_bits[1:] + view_bits[1:])
     levels = len(orders[0])
     n_halved = min(HALVINGS, levels - 1)
     n_exchanged = levels - n_halved
@@ -343,7 +340,7 @@
             jax.ShapeDtypeStruct((rows, features), BF),
             jax.ShapeDtypeStruct((rows, features), BF),
             jax.ShapeDtypeStruct((rows, features), BF),
-            jax.ShapeDtypeStruct((rows, 1), F32),
+            jax.ShapeDtypeStruct((1, rows), F32),
         ),
         in_specs=[vmem] * 8,
         out_specs=(vmem,) * 4,
@@ -366,7 +363,13 @@
         compiler_params=pltpu.CompilerParams(
             collective_id=0, has_side_effects=True, vmem_limit_bytes=60 * 1024 * 1024
         ),
-    )(q, k, v, r.reshape(rows, 1), o, wg, wu, wd)
+    )(q, k, v, r.reshape(1, rows), o, wg, wu, wd)
+    outs = pl.pallas_call(
+        handing,
+        out_shape=tuple(jax.ShapeDtypeStruct(out.shape, out.dtype) for out in outs),
+        in_specs=[vmem] * 4,
+        out_specs=(vmem,) * 4,
+    )(*outs)
     return (outs[0], outs[1], outs[2], outs[3].reshape(rows))
 
 

time: 93.6 us -> 80.9 us (0.86)
  local copies, waits for them, and re-layouts: 6.34 us -> 0 us
  Pallas kernels: 84.8 us -> 80.1 us
  other arithmetic: 1.58 us -> 0 us
    pallas_call x1, Pallas kernels: 84.8 us -> 78.2 us  [on_device(): pl.pallas_call(functools.partial(kernel, orders, n_halved, n_exchanged),...]
    unnamed x3 -> x0, local copies, waits for them, and re-layouts: 4.87 us -> none
    pallas_call x0 -> x1, Pallas kernels: none -> 1.95 us  [on_device(): pl.pallas_call(handing, out_shape=tuple((jax.ShapeDtypeStruct(out.shape,...]
    pallas_call x1 -> x0, other arithmetic: 1.58 us -> none  [on_device(): pl.pallas_call(functools.partial(kernel, orders, n_halved, n_exchanged),...]
    reshape x1 -> x0, local copies, waits for them, and re-layouts: 1.47 us -> none  [on_device(): r.reshape(rows, 1)]
where the time goes in v2:
time: 80.9 us; the launch traced here: 80.8 us
  Pallas kernels  80.1 us (99%)
    pallas_call x1, Pallas kernels, on_device(): pl.pallas_call(functools.partial(kernel, orders, n_halved, n_exchanged),...  78.2 us
    pallas_call x1, Pallas kernels, on_device(): pl.pallas_call(handing, out_shape=tuple((jax.ShapeDtypeStruct(out.shape,...  1.95 us

profile of v2, /device:TPU:0, one launch (start us, length us, event | category | flops | bytes accessed | tf_op | source)
XLA Modules:
  0.0 80.8 jit_solution(4995868997822098241)
XLA Ops:
  0.6 78.2 %shard_map.111 = (bf16[256,384]{1,0:T(8,128)(2,1)}, bf16[256,384]{1,0:T(8,128)(2,1)}, bf16[256,384]{1,0:T(8,128)(2,1)}, f32[1,256]{1,0:T(1,128)}) custom-call(bf16[256,384]{1,0:T(8,128)(2,1)} %q_ref.1, bf16[256,384]{1,0:T(8,128)(2,1)} %k_ref.1, bf16[256,384]{1,0:T(8,128)(2,1)} %v_ref.1, f32[1,256]{1,0:T(1,128)} %bitcast.2, bf16[256,384]{1,0:T(8,128)(2,1)} %o_ref.1, ...), custom_call_target="tpu_custom_call" | custom-call | tf_op jit(solution)/shard_map/pallas_call | solution.py:337
  78.8 1.9 %shard_map.112 = (bf16[256,384]{1,0:T(8,128)(2,1)}, bf16[256,384]{1,0:T(8,128)(2,1)}, bf16[256,384]{1,0:T(8,128)(2,1)}, f32[1,256]{1,0:T(1,128)}) custom-call(bf16[256,384]{1,0:T(8,128)(2,1)} %get-tuple-element.12.refs_0_, bf16[256,384]{1,0:T(8,128)(2,1)} %get-tuple-element.13.refs_1_, bf16[256,384]{1,0:T(8,128)(2,1)} %get-tuple-element.14.refs_2_, ...), custom_call_target="tpu_custom_call" | custom-call | tf_op jit(solution)/shard_map/pallas_call | solution.py:367

commit v3 on v2

--- a/solution.py
+++ b/solution.py
@@ -158,7 +158,7 @@
             every.append(chunk)
 
     def pump(number, matrix):
-        for half in range(halves):
+        for half in reversed(range(halves)):
             chunk = chunks[number, matrix, half]
             if chunk.step <= chunk.steps:
                 chunk.advance()

time: 80.9 us -> 79.3 us (0.980)
  Pallas kernels: 80.1 us -> 78.5 us
    pallas_call x1, Pallas kernels: 78.2 us -> 76.5 us  [on_device(): pl.pallas_call(functools.partial(kernel, orders, n_halved, n_exchanged),...]
where the time goes in v3:
time: 79.3 us; the launch traced here: 79.1 us
  Pallas kernels  78.5 us (99%)
    pallas_call x1, Pallas kernels, on_device(): pl.pallas_call(functools.partial(kernel, orders, n_halved, n_exchanged),...  76.5 us
    pallas_call x1, Pallas kernels, on_device(): pl.pallas_call(handing, out_shape=tuple((jax.ShapeDtypeStruct(out.shape,...  1.95 us

profile of v3, /device:TPU:0, one launch (start us, length us, event | category | flops | bytes accessed | tf_op | source)
XLA Modules:
  0.0 79.1 jit_solution(3361883946785403483)
XLA Ops:
  0.6 76.5 %shard_map.111 = (bf16[256,384]{1,0:T(8,128)(2,1)}, bf16[256,384]{1,0:T(8,128)(2,1)}, bf16[256,384]{1,0:T(8,128)(2,1)}, f32[1,256]{1,0:T(1,128)}) custom-call(bf16[256,384]{1,0:T(8,128)(2,1)} %q_ref.1, bf16[256,384]{1,0:T(8,128)(2,1)} %k_ref.1, bf16[256,384]{1,0:T(8,128)(2,1)} %v_ref.1, f32[1,256]{1,0:T(1,128)} %bitcast.2, bf16[256,384]{1,0:T(8,128)(2,1)} %o_ref.1, ...), custom_call_target="tpu_custom_call" | custom-call | tf_op jit(solution)/shard_map/pallas_call | solution.py:337
  77.2 1.9 %shard_map.112 = (bf16[256,384]{1,0:T(8,128)(2,1)}, bf16[256,384]{1,0:T(8,128)(2,1)}, bf16[256,384]{1,0:T(8,128)(2,1)}, f32[1,256]{1,0:T(1,128)}) custom-call(bf16[256,384]{1,0:T(8,128)(2,1)} %get-tuple-element.12.refs_0_, bf16[256,384]{1,0:T(8,128)(2,1)} %get-tuple-element.13.refs_1_, bf16[256,384]{1,0:T(8,128)(2,1)} %get-tuple-element.14.refs_2_, ...), custom_call_target="tpu_custom_call" | custom-call | tf_op jit(solution)/shard_map/pallas_call | solution.py:367
